TPU v7x, 128 devices: a whole 4x4x4 slice. The times are simulated.
128 devices in a mesh: ctx: 128 (over y, z, x, core).
Axes of the slice: x: 4, y: 4, z: 4, core: 2. Of those that a mesh axis runs over, the one named last changes fastest.
Arguments:
- query_rows: bfloat16 [32768, 32, 128], P('ctx'), may hold values from -6 to 6
- key_rows: bfloat16 [32768, 16, 128], P('ctx'), may hold values from -6 to 6
- value_rows: bfloat16 [32768, 16, 128], P('ctx'), may hold values from -6 to 6
- grad_out: bfloat16 [4096, 32768], P('ctx'), may hold values from -6 to 6
Outputs:
- grad_query: bfloat16 [32768, 32, 128], P('ctx')
- grad_key: bfloat16 [32768, 16, 128], P('ctx')
- grad_value: bfloat16 [32768, 16, 128], P('ctx')
All inputs are finite; a program needn't handle non-finite values.
Results may differ from a plain program's by a relative error of at most 0.019.
Values may be sent and summed in bfloat16 or wider, within the bound.
A program may use at most 128 MiB of HBM per device.

v0:
```python
from functools import partial

import jax
import jax.numpy as jnp
from jax import lax
from jax.sharding import PartitionSpec as P

W = 1024


query_scale = 1.0 / 12.0


def from_behind(value, axis, by):
    count = lax.axis_size(axis)
    pairs = [(i, i + by) for i in range(count) if 0 <= i + by < count]
    return lax.ppermute(value, axis, pairs)


def head_pass(allowed, inputs):
    q_group, k_window, v_window, do_group = inputs
    scores = (
        jnp.einsum("thd,kd->htk", q_group, k_window, preferred_element_type=jnp.float32)
        * query_scale
    )
    masked = jnp.where(allowed, scores, -1e30)
    top = jnp.max(masked, axis=-1, keepdims=True)
    weights = jnp.exp(masked - top)
    probs = (weights / jnp.sum(weights, axis=-1, keepdims=True)).astype(jnp.bfloat16)
    dprobs = jnp.einsum("hdt,kd->htk", do_group, v_window, preferred_element_type=jnp.float32)
    probs_wide = probs.astype(jnp.float32)
    delta = jnp.sum(probs_wide * dprobs, axis=-1, keepdims=True)
    dscores = (probs_wide * (dprobs - delta) * query_scale).astype(jnp.bfloat16)
    dq_group = jnp.einsum(
        "htk,kd->thd", dscores, k_window, preferred_element_type=jnp.float32
    ).astype(jnp.bfloat16)
    dv_window = jnp.einsum(
        "htk,hdt->kd", probs, do_group, preferred_element_type=jnp.float32
    ).astype(jnp.bfloat16)
    dk_window = jnp.einsum(
        "htk,thd->kd", dscores, q_group, preferred_element_type=jnp.float32
    ).astype(jnp.bfloat16)
    return (dq_group, dk_window, dv_window)


def on_device(query_rows, key_rows, value_rows, grad_out):
    tokens = query_rows.shape[0]
    heads_kv = key_rows.shape[1]
    depth = key_rows.shape[2]
    slabs = W // tokens
    gathered = lax.all_to_all(grad_out, "ctx", split_axis=1, concat_axis=0, tiled=True)
    grad_heads = gathered.reshape(heads_kv, 2, depth, tokens)
    own_keys = jnp.transpose(key_rows, (1, 0, 2))
    own_values = jnp.transpose(value_rows, (1, 0, 2))
    pieces = [None] * slabs
    for offset in range(1, slabs + 1):
        pieces[slabs - offset] = from_behind((own_keys, own_values), "ctx", offset)
    window_keys = jnp.concatenate([piece[0] for piece in pieces] + [own_keys], axis=1)
    window_values = jnp.concatenate([piece[1] for piece in pieces] + [own_values], axis=1)
    start = lax.axis_index("ctx") * tokens
    row_pos = jnp.arange(tokens, dtype=jnp.int32)[:, None]
    col_pos = jnp.arange(W + tokens, dtype=jnp.int32)[None, :]
    allowed = (col_pos > row_pos) & (col_pos <= row_pos + W) & (start - W + col_pos >= 0)
    query_heads = jnp.transpose(query_rows.reshape(tokens, heads_kv, 2, depth), (1, 0, 2, 3))
    dq_heads, dk_window, dv_window = lax.map(
        partial(head_pass, allowed), (query_heads, window_keys, window_values, grad_heads)
    )
    grad_query = jnp.transpose(dq_heads, (1, 0, 2, 3)).reshape(tokens, 2 * heads_kv, depth)

    def slab_of(array, index):
        return array[:, index * tokens : (index + 1) * tokens]

    total_key = slab_of(dk_window, slabs).astype(jnp.float32)
    total_value = slab_of(dv_window, slabs).astype(jnp.float32)
    for offset in range(1, slabs + 1):
        far_key, far_value = from_behind(
            (slab_of(dk_window, slabs - offset), slab_of(dv_window, slabs - offset)), "ctx", -offset
        )
        total_key = total_key + far_key.astype(jnp.float32)
        total_value = total_value + far_value.astype(jnp.float32)
    grad_key = jnp.transpose(total_key, (1, 0, 2)).astype(jnp.bfloat16)
    grad_value = jnp.transpose(total_value, (1, 0, 2)).astype(jnp.bfloat16)
    return (grad_query, grad_key, grad_value)


def solution(mesh):
    in_specs = (P("ctx", None, None), P("ctx", None, None), P("ctx", None, None), P("ctx", None))
    out_specs = (P("ctx", None, None), P("ctx", None, None), P("ctx", None, None))
    return jax.shard_map(
        on_device, mesh=mesh, in_specs=in_specs, out_specs=out_specs, check_vma=False
    )
```

profile of v0, /device:TPU:7, one launch (start us, length us, event | category | flops | bytes accessed | tf_op | source)
XLA Modules:
  0.0 682.8 jit_solution(6825160904747708585)
XLA Ops:
  3.3 4.4 collective-permute-start.4
  8.9 4.6 collective-permute-start.1
  13.5 4.4 collective-permute-start
  25.5 8.1 %all-to-all-start = ((bf16[32,128,256]{2,0,1:T(8,128)(2,1)}), bf16[32,128,256]{2,0,1:T(8,128)(2,1)S(1)}, u32[]{:S(2)}, u32[]{:S(2)}) async-start(bf16[32,128,256]{2,0,1:T(8,128)(2,1)} %bitcast.101), calls=%async_computation | async-start | bytes 4194304 | tf_op jit(solution)/shard_map/all_to_all | solution.py:51
  33.6 5.3 collective-permute-start.5
  42.7 17.1 %collective-permute-done.1 = bf16[16,256,128]{2,1,0:T(8,128)(2,1)} collective-permute-done((bf16[16,256,128]{2,1,0:T(8,128)(2,1)}, bf16[16,256,128]{2,1,0:T(8,128)(2,1)}, u32[]{:S(2)}, u32[]{:S(2)}) %collective-permute-start.1) | collective-permute-done | bytes 1048608 | tf_op jit(solution)/shard_map/ppermute | solution.py:17
  59.8 42.4 %collective-permute-start.6 = (bf16[16,256,128]{2,1,0:T(8,128)(2,1)}, bf16[16,256,128]{2,1,0:T(8,128)(2,1)S(1)}, u32[]{:S(2)}, u32[]{:S(2)}) collective-permute-start(bf16[16,256,128]{2,1,0:T(8,128)(2,1)} %bitcast.102), channel_id=1, source_target_pairs={{0,2},{1,3},{2,4},{3,5},{4,6},{5,7},{6,8},{7,9},{8,10},{9,11},{10,... | collective-permute-start | bytes 3145736 | tf_op jit(solution)/shard_map/ppermute | solution.py:17
  110.7 14.4 %collective-permute-done.3 = bf16[16,256,128]{2,1,0:T(8,128)(2,1)} collective-permute-done((bf16[16,256,128]{2,1,0:T(8,128)(2,1)}, bf16[16,256,128]{2,1,0:T(8,128)(2,1)}, u32[]{:S(2)}, u32[]{:S(2)}) %collective-permute-start.3) | collective-permute-done | bytes 1048608 | tf_op jit(solution)/shard_map/ppermute | solution.py:17
  126.6 20.6 %collective-permute-done.5 = bf16[16,256,128]{2,1,0:T(8,128)(2,1)} collective-permute-done((bf16[16,256,128]{2,1,0:T(8,128)(2,1)}, bf16[16,256,128]{2,1,0:T(8,128)(2,1)}, u32[]{:S(2)}, u32[]{:S(2)}) %collective-permute-start.5) | collective-permute-done | bytes 1048608 | tf_op jit(solution)/shard_map/ppermute | solution.py:17
  149.6 29.8 %collective-permute-done.6 = bf16[16,256,128]{2,1,0:T(8,128)(2,1)S(1)} collective-permute-done((bf16[16,256,128]{2,1,0:T(8,128)(2,1)}, bf16[16,256,128]{2,1,0:T(8,128)(2,1)S(1)}, u32[]{:S(2)}, u32[]{:S(2)}) %collective-permute-start.6) | collective-permute-done | bytes 1048608 | tf_op jit(solution)/shard_map/ppermute | solution.py:17
  180.6 17.7 %collective-permute-done.7 = bf16[16,256,128]{2,1,0:T(8,128)(2,1)S(1)} collective-permute-done((bf16[16,256,128]{2,1,0:T(8,128)(2,1)}, bf16[16,256,128]{2,1,0:T(8,128)(2,1)S(1)}, u32[]{:S(2)}, u32[]{:S(2)}) %collective-permute-start.7) | collective-permute-done | bytes 1048608 | tf_op jit(solution)/shard_map/ppermute | solution.py:17
  203.3 291.8 %while.15 = (s32[]{:T(128)}, bf16[16,256,2,128]{1,3,2,0:T(8,128)(2,1)}, bf16[16,1280,128]{2,1,0:T(8,128)(2,1)}, bf16[16,1280,128]{2,1,0:T(8,128)(2,1)}, bf16[16,...) while((s32[]{:T(128)}, ...), condition=%wide.region_4.5_spmd.clone, body=%wide.region_0.4_spmd.clone.sunk | while | flops 853676800 | bytes 29175156 | solution.py:65
  266.7 4.2 fusion.101
  284.9 4.2 fusion.101
  376.1 4.2 fusion.101
  394.4 4.2 fusion.101
  485.6 4.2 fusion.101
  495.1 14.7 %copy.83 = bf16[16,1280,128]{2,0,1:T(8,128)(2,1)S(1)} copy(bf16[16,1280,128]{2,1,0:T(8,128)(2,1)} %get-tuple-element.54) | data formatting | bytes 10485760 | tf_op jit(solution)/shard_map/while | solution.py:65
  521.7 14.3 %copy.78 = bf16[16,1280,128]{2,0,1:T(8,128)(2,1)S(1)} copy(bf16[16,1280,128]{2,1,0:T(8,128)(2,1)S(1)} %bitcast.134) | data formatting | bytes 10485760 | tf_op jit(solution)/shard_map/while | solution.py:65
  541.6 34.7 %collective-permute-done.12 = bf16[16,256,128]{2,0,1:T(8,128)(2,1)S(1)} collective-permute-done((bf16[16,256,128]{2,0,1:T(8,128)(2,1)S(1)}, bf16[16,256,128]{2,0,1:T(8,128)(2,1)S(1)}, u32[]{:S(2)}, u32[]{:S(2)}) %collective-permute-start.12) | collective-permute-done | bytes 1048608 | tf_op jit(solution)/shard_map/ppermute | solution.py:17
  586.0 26.6 %collective-permute-done.13 = bf16[16,256,128]{2,0,1:T(8,128)(2,1)} collective-permute-done((bf16[16,256,128]{2,0,1:T(8,128)(2,1)}, bf16[16,256,128]{2,0,1:T(8,128)(2,1)}, u32[]{:S(2)}, u32[]{:S(2)}) %collective-permute-start.13) | collective-permute-done | bytes 1048608 | tf_op jit(solution)/shard_map/ppermute | solution.py:17
  616.5 35.2 %collective-permute-done.8 = bf16[16,256,128]{2,0,1:T(8,128)(2,1)} collective-permute-done((bf16[16,256,128]{2,0,1:T(8,128)(2,1)}, bf16[16,256,128]{2,0,1:T(8,128)(2,1)}, u32[]{:S(2)}, u32[]{:S(2)}) %collective-permute-start.8) | collective-permute-done | bytes 1048608 | tf_op jit(solution)/shard_map/ppermute | solution.py:17
  651.7 5.9 collective-permute-done.10
  657.6 21.0 %collective-permute-done.9 = bf16[16,256,128]{2,0,1:T(8,128)(2,1)} collective-permute-done((bf16[16,256,128]{2,0,1:T(8,128)(2,1)}, bf16[16,256,128]{2,0,1:T(8,128)(2,1)}, u32[]{:S(2)}, u32[]{:S(2)}) %collective-permute-start.9) | collective-permute-done | bytes 1048608 | tf_op jit(solution)/shard_map/ppermute | solution.py:17
  (168 shorter events, 339.5 us)
Async XLA Ops:
  0.6 7.0 %copy-start.2 = (bf16[256,16,128]{2,1,0:T(8,128)(2,1)S(1)}, bf16[256,16,128]{2,1,0:T(8,128)(2,1)}, u32[]{:S(2)}) copy-start(bf16[256,16,128]{2,1,0:T(8,128)(2,1)} %param.7) | copy-start | bytes 3145732
  0.6 23.2 %copy-start.4 = (bf16[32,32768]{1,0:T(8,128)(2,1)S(1)}, bf16[32,32768]{1,0:T(8,128)(2,1)}, u32[]{:S(2)}) copy-start(bf16[32,32768]{1,0:T(8,128)(2,1)} %param.9) | copy-start | bytes 6291460
  3.3 30.3 %collective-permute-start.4 = (bf16[16,256,128]{2,1,0:T(8,128)(2,1)}, bf16[16,256,128]{2,1,0:T(8,128)(2,1)}, u32[]{:S(2)}, u32[]{:S(2)}) collective-permute-start(bf16[16,256,128]{2,1,0:T(8,128)(2,1)} %bitcast.102), channel_id=1, source_target_pairs={{0,4},{1,5},{2,6},{3,7},{4,8},{5,9},{6,10},{7,11},{8,12},{9,13},{1... | collective-permute-start | bytes 3145736 | tf_op jit(solution)/shard_map/ppermute | solution.py:17
  8.9 50.9 %collective-permute-start.1 = (bf16[16,256,128]{2,1,0:T(8,128)(2,1)}, bf16[16,256,128]{2,1,0:T(8,128)(2,1)}, u32[]{:S(2)}, u32[]{:S(2)}) collective-permute-start(bf16[16,256,128]{2,1,0:T(8,128)(2,1)} %bitcast.103), channel_id=1, source_target_pairs={{0,3},{1,4},{2,5},{3,6},{4,7},{5,8},{6,9},{7,10},{8,11},{9,12},{10... | collective-permute-start | bytes 3145736 | tf_op jit(solution)/shard_map/ppermute | solution.py:17
  13.5 88.7 %collective-permute-start = (bf16[16,256,128]{2,1,0:T(8,128)(2,1)}, bf16[16,256,128]{2,1,0:T(8,128)(2,1)}, u32[]{:S(2)}, u32[]{:S(2)}) collective-permute-start(bf16[16,256,128]{2,1,0:T(8,128)(2,1)} %bitcast.103), channel_id=1, source_target_pairs={{0,4},{1,5},{2,6},{3,7},{4,8},{5,9},{6,10},{7,11},{8,12},{9,13},{1... | collective-permute-start | bytes 3145736 | tf_op jit(solution)/shard_map/ppermute | solution.py:17
  17.9 91.4 %collective-permute-start.2 = (bf16[16,256,128]{2,1,0:T(8,128)(2,1)}, bf16[16,256,128]{2,1,0:T(8,128)(2,1)}, u32[]{:S(2)}, u32[]{:S(2)}) collective-permute-start(bf16[16,256,128]{2,1,0:T(8,128)(2,1)} %bitcast.103), channel_id=1, source_target_pairs={{0,2},{1,3},{2,4},{3,5},{4,6},{5,7},{6,8},{7,9},{8,10},{9,11},{10,... | collective-permute-start | bytes 3145736 | tf_op jit(solution)/shard_map/ppermute | solution.py:17
  21.6 103.5 %collective-permute-start.3 = (bf16[16,256,128]{2,1,0:T(8,128)(2,1)}, bf16[16,256,128]{2,1,0:T(8,128)(2,1)}, u32[]{:S(2)}, u32[]{:S(2)}) collective-permute-start(bf16[16,256,128]{2,1,0:T(8,128)(2,1)} %bitcast.103), channel_id=1, source_target_pairs={{0,1},{1,2},{2,3},{3,4},{4,5},{5,6},{6,7},{7,8},{8,9},{9,10},{10,1... | collective-permute-start | bytes 3145736 | tf_op jit(solution)/shard_map/ppermute | solution.py:17
  25.5 177.8 %all-to-all-start = ((bf16[32,128,256]{2,0,1:T(8,128)(2,1)}), bf16[32,128,256]{2,0,1:T(8,128)(2,1)S(1)}, u32[]{:S(2)}, u32[]{:S(2)}) async-start(bf16[32,128,256]{2,0,1:T(8,128)(2,1)} %bitcast.101), calls=%async_computation | async-start | bytes 4194304 | tf_op jit(solution)/shard_map/all_to_all | solution.py:51
  33.6 113.6 %collective-permute-start.5 = (bf16[16,256,128]{2,1,0:T(8,128)(2,1)}, bf16[16,256,128]{2,1,0:T(8,128)(2,1)}, u32[]{:S(2)}, u32[]{:S(2)}) collective-permute-start(bf16[16,256,128]{2,1,0:T(8,128)(2,1)} %bitcast.102), channel_id=1, source_target_pairs={{0,3},{1,4},{2,5},{3,6},{4,7},{5,8},{6,9},{7,10},{8,11},{9,12},{10... | collective-permute-start | bytes 3145736 | tf_op jit(solution)/shard_map/ppermute | solution.py:17
  59.8 119.6 %collective-permute-start.6 = (bf16[16,256,128]{2,1,0:T(8,128)(2,1)}, bf16[16,256,128]{2,1,0:T(8,128)(2,1)S(1)}, u32[]{:S(2)}, u32[]{:S(2)}) collective-permute-start(bf16[16,256,128]{2,1,0:T(8,128)(2,1)} %bitcast.102), channel_id=1, source_target_pairs={{0,2},{1,3},{2,4},{3,5},{4,6},{5,7},{6,8},{7,9},{8,10},{9,11},{10,... | collective-permute-start | bytes 3145736 | tf_op jit(solution)/shard_map/ppermute | solution.py:17
  102.2 96.0 %collective-permute-start.7 = (bf16[16,256,128]{2,1,0:T(8,128)(2,1)}, bf16[16,256,128]{2,1,0:T(8,128)(2,1)S(1)}, u32[]{:S(2)}, u32[]{:S(2)}) collective-permute-start(bf16[16,256,128]{2,1,0:T(8,128)(2,1)} %bitcast.102), channel_id=1, source_target_pairs={{0,1},{1,2},{2,3},{3,4},{4,5},{5,6},{6,7},{7,8},{8,9},{9,10},{10,1... | collective-permute-start | bytes 3145736 | tf_op jit(solution)/shard_map/ppermute | solution.py:17
  180.6 21.5 %copy-start.3 = (bf16[256,16,128]{2,1,0:T(8,128)(2,1)S(1)}, bf16[256,16,128]{2,1,0:T(8,128)(2,1)}, u32[]{:S(2)}) copy-start(bf16[256,16,128]{2,1,0:T(8,128)(2,1)} %param.8) | copy-start | bytes 3145732
  495.1 26.5 %slice-start = ((s8[5242880]{0:T(1024)(128)(4,1)}), s8[4194304]{0:T(1024)(128)(4,1)S(1)}, s32[]{:S(2)}) async-start(s8[5242880]{0:T(1024)(128)(4,1)} %bitcast.133), calls=%async_computation.1 | async-start | bytes 8388608
  495.1 26.5 %slice-start.1 = ((s8[5242880]{0:T(1024)(128)(4,1)}), s8[1048576]{0:T(1024)(128)(4,1)S(1)}, s32[]{:S(2)}) async-start(s8[5242880]{0:T(1024)(128)(4,1)} %bitcast.133), calls=%async_computation.2 | async-start | bytes 2097152
  512.5 63.8 %collective-permute-start.12 = (bf16[16,256,128]{2,0,1:T(8,128)(2,1)S(1)}, bf16[16,256,128]{2,0,1:T(8,128)(2,1)S(1)}, u32[]{:S(2)}, u32[]{:S(2)}) collective-permute-start(bf16[16,256,128]{2,0,1:T(8,128)(2,1)S(1)} %get-tuple-element.131), channel_id=1, source_target_pairs={{1,0},{2,1},{3,2},{4,3},{5,4},{6,5},{7,6},{8,7},{9,8},{10,9},{11,1... | collective-permute-start | bytes 3145736 | tf_op jit(solution)/shard_map/ppermute | solution.py:17
  515.8 62.4 %collective-permute-start.15 = (bf16[16,256,128]{2,0,1:T(8,128)(2,1)S(1)}, bf16[16,256,128]{2,0,1:T(8,128)(2,1)}, u32[]{:S(2)}, u32[]{:S(2)}) collective-permute-start(bf16[16,256,128]{2,0,1:T(8,128)(2,1)S(1)} %get-tuple-element.132), channel_id=1, source_target_pairs={{4,0},{5,1},{6,2},{7,3},{8,4},{9,5},{10,6},{11,7},{12,8},{13,9},{1... | collective-permute-start | bytes 3145736 | tf_op jit(solution)/shard_map/ppermute | solution.py:17
  517.8 62.4 %collective-permute-start.14 = (bf16[16,256,128]{2,0,1:T(8,128)(2,1)S(1)}, bf16[16,256,128]{2,0,1:T(8,128)(2,1)}, u32[]{:S(2)}, u32[]{:S(2)}) collective-permute-start(bf16[16,256,128]{2,0,1:T(8,128)(2,1)S(1)} %get-tuple-element.133), channel_id=1, source_target_pairs={{3,0},{4,1},{5,2},{6,3},{7,4},{8,5},{9,6},{10,7},{11,8},{12,9},{13... | collective-permute-start | bytes 3145736 | tf_op jit(solution)/shard_map/ppermute | solution.py:17
  519.7 93.0 %collective-permute-start.13 = (bf16[16,256,128]{2,0,1:T(8,128)(2,1)}, bf16[16,256,128]{2,0,1:T(8,128)(2,1)}, u32[]{:S(2)}, u32[]{:S(2)}) collective-permute-start(bf16[16,256,128]{2,0,1:T(8,128)(2,1)} %get-tuple-element.134), channel_id=1, source_target_pairs={{2,0},{3,1},{4,2},{5,3},{6,4},{7,5},{8,6},{9,7},{10,8},{11,9},{12,... | collective-permute-start | bytes 3145736 | tf_op jit(solution)/shard_map/ppermute | solution.py:17
  535.9 3.8 copy-start.1
  535.9 46.2 %copy-start.5 = (bf16[16,256,2,128]{1,3,2,0:T(8,128)(2,1)S(1)}, bf16[16,256,2,128]{1,3,2,0:T(8,128)(2,1)}, u32[]{:S(2)}) copy-start(bf16[16,256,2,128]{1,3,2,0:T(8,128)(2,1)} %get-tuple-element.52) | copy-start | bytes 6291460
  539.7 112.0 %collective-permute-start.8 = (bf16[16,256,128]{2,0,1:T(8,128)(2,1)}, bf16[16,256,128]{2,0,1:T(8,128)(2,1)}, u32[]{:S(2)}, u32[]{:S(2)}) collective-permute-start(bf16[16,256,128]{2,0,1:T(8,128)(2,1)} %get-tuple-element.135), channel_id=1, source_target_pairs={{1,0},{2,1},{3,2},{4,3},{5,4},{6,5},{7,6},{8,7},{9,8},{10,9},{11,1... | collective-permute-start | bytes 3145736 | tf_op jit(solution)/shard_map/ppermute | solution.py:17
  576.3 75.4 %collective-permute-start.11 = (bf16[16,256,128]{2,0,1:T(8,128)(2,1)}, bf16[16,256,128]{2,0,1:T(8,128)(2,1)}, u32[]{:S(2)}, u32[]{:S(2)}) collective-permute-start(bf16[16,256,128]{2,0,1:T(8,128)(2,1)} %get-tuple-element.136), channel_id=1, source_target_pairs={{4,0},{5,1},{6,2},{7,3},{8,4},{9,5},{10,6},{11,7},{12,8},{13,9},{1... | collective-permute-start | bytes 3145736 | tf_op jit(solution)/shard_map/ppermute | solution.py:17
  578.2 79.4 %collective-permute-start.10 = (bf16[16,256,128]{2,0,1:T(8,128)(2,1)}, bf16[16,256,128]{2,0,1:T(8,128)(2,1)}, u32[]{:S(2)}, u32[]{:S(2)}) collective-permute-start(bf16[16,256,128]{2,0,1:T(8,128)(2,1)} %get-tuple-element.137), channel_id=1, source_target_pairs={{3,0},{4,1},{5,2},{6,3},{7,4},{8,5},{9,6},{10,7},{11,8},{12,9},{13... | collective-permute-start | bytes 3145736 | tf_op jit(solution)/shard_map/ppermute | solution.py:17
  580.2 98.4 %collective-permute-start.9 = (bf16[16,256,128]{2,0,1:T(8,128)(2,1)}, bf16[16,256,128]{2,0,1:T(8,128)(2,1)}, u32[]{:S(2)}, u32[]{:S(2)}) collective-permute-start(bf16[16,256,128]{2,0,1:T(8,128)(2,1)} %get-tuple-element.138), channel_id=1, source_target_pairs={{2,0},{3,1},{4,2},{5,3},{6,4},{7,5},{8,6},{9,7},{10,8},{11,9},{12,... | collective-permute-start | bytes 3145736 | tf_op jit(solution)/shard_map/ppermute | solution.py:17
  (2 other events, 5.0 us)
where the time goes:
time: 686 us; the launch traced here: 683 us
  matrix products  255 us (37%)
  waiting for transfers between devices  223 us (33%)
  starting transfers between devices  93.7 us (14%)
  local copies, waits for them, and re-layouts  65.2 us (10%)
  other arithmetic  44.5 us (6%)
    ppermute x16, waiting for transfers between devices, from_behind(): return lax.ppermute(value, axis, pairs)  223 us
    ppermute x16, starting transfers between devices, from_behind(): return lax.ppermute(value, axis, pairs)  85.6 us
    dot_general x16, matrix products, head_pass(): jnp.einsum('htk,kd->thd', dscores, k_window, preferred_element_type=jnp.f...  66.8 us
    dot_general x16, matrix products, head_pass(): jnp.einsum('htk,thd->kd', dscores, q_group, preferred_element_type=jnp.fl...  65.6 us
    sub x16, matrix products, head_pass(): weights = jnp.exp(masked - top)  55.3 us
    dot_general x16, matrix products, head_pass(): jnp.einsum('hdt,kd->htk', do_group, v_window, preferred_element_type=jnp....  47.7 us
    convert_element_type x16, other arithmetic, head_pass(): (weights / jnp.sum(weights, axis=-1, keepdims=True)).astype(jnp.bfloat16)  31.3 us
    while x2, local copies, waits for them, and re-layouts, on_device(): lax.map(partial(head_pass, allowed), (query_heads, window_keys, window_va...  29 us
  transfers between devices with their start and end apart: 17, of which 10 were waited for; matrix products, arithmetic and copies ran while one was open for 7% of the time, Pallas kernels for 0%

commit v1 on v0

v1 whole, which is shorter than its diff:
```python
import functools

import jax
import jax.numpy as jnp
from jax import lax
from jax.experimental import pallas as pl
from jax.experimental.pallas import tpu as pltpu
from jax.sharding import PartitionSpec as P

MESH = pl.DeviceIdType.MESH
SCALE = 1.0 / 12.0
LOG2E = 1.4426950408889634
T = 256
D = 128
HK = 8
NEG = -1e30

NT = (((1,), (1,)), ((), ()))
TN = (((0,), (0,)), ((), ()))


def dot(a, b, dims=(((1,), (0,)), ((), ()))):
    return lax.dot_general(a, b, dims, preferred_element_type=jnp.float32)


def attend(i, first, kv, q, do, s_scr, p_scr, g_scr, ds_scr, acc, dq):
    row = lax.broadcasted_iota(jnp.int32, (T, T), 0)
    col = lax.broadcasted_iota(jnp.int32, (T, T), 1)
    after = row > col
    after = jnp.concatenate([after, after], axis=1)
    for b in range(2):
        qb = q[b, pl.ds(2 * i, 2)].reshape(2 * T, D)
        dob = jnp.concatenate(
            [do[2 * i, :, b * T : (b + 1) * T], do[2 * i + 1, :, b * T : (b + 1) * T]], axis=1
        )
        tops = []
        for j in range(5):
            rows = pl.ds((b + j) * T, T)
            s = dot(kv[i, 0, rows, :], qb, NT)
            if j == 0:
                s = jnp.where(after, s, NEG)
            if j == 4:
                s = jnp.where(after, NEG, s)
            s_scr[pl.ds(j * T, T), :] = s
            t = jnp.max(s, axis=0, keepdims=True)
            if j < 4:
                t = jnp.where(first + b + j >= 0, t, NEG)
            tops.append(t)
        top = functools.reduce(jnp.maximum, tops)
        total = jnp.zeros((1, 2 * T), jnp.float32)
        delta = jnp.zeros((1, 2 * T), jnp.float32)
        for j in range(5):
            rows = pl.ds((b + j) * T, T)
            here = pl.ds(j * T, T)
            t = top
            if j < 4:
                t = jnp.where(first + b + j >= 0, top, -NEG)
            p = jnp.exp2((s_scr[here, :] - t) * (SCALE * LOG2E))
            g = dot(kv[i, 1, rows, :], dob)
            total = total + jnp.sum(p, axis=0, keepdims=True)
            delta = delta + jnp.sum(p * g, axis=0, keepdims=True)
            p_scr[here, :] = p
            g_scr[here, :] = g
        inv = 1.0 / total
        delta = delta * inv
        for j in range(5):
            rows = pl.ds((b + j) * T, T)
            here = pl.ds(j * T, T)
            p = p_scr[here, :] * inv
            ds = (p * (g_scr[here, :] - delta)).astype(jnp.bfloat16)
            ds_scr[here, :] = ds
            dv = dot(p.astype(jnp.bfloat16), dob, NT)
            dk = dot(ds, qb) * SCALE
            if b == 0 or j == 4:
                acc[i, 0, rows, :] = dk
                acc[i, 1, rows, :] = dv
            else:
                acc[i, 0, rows, :] += dk
                acc[i, 1, rows, :] += dv
        dqt = dot(kv[i, 0, pl.ds(b * T, 5 * T), :], ds_scr[...], TN)
        dq[b, pl.ds(2 * i, 2)] = (
            (jnp.transpose(dqt) * SCALE).astype(jnp.bfloat16).reshape(2, T, D)
        )


def kernel(
    n, q_in, k_in, v_in, do_in, dq_out, dkv_out,
    kv, q, do, dq, s_scr, p_scr, g_scr, ds_scr, acc,
    part_a, got_a, part_b, got_b, fin,
    loc_sem, d2d_send, d2d_recv, fb_send, fb_recv, fa_send, fa_recv,
    ra_send, ra_recv, rb_send, rb_recv, out_loc, out_send, out_recv,
):
    me = lax.axis_index("ctx")
    core = lax.rem(me, 2)
    chip = me // 2
    sib = 2 * chip + (1 - core)
    nxt = lax.rem(me + 2, n)
    prv = lax.rem(me + n - 2, n)

    barrier = pltpu.get_barrier_semaphore()
    for other in (sib, nxt, prv):
        pl.semaphore_signal(barrier, inc=1, device_id=(other,), device_id_type=MESH)
    pl.semaphore_wait(barrier, 3)

    def remote(src, dst, send, recv, dev):
        return pltpu.make_async_remote_copy(
            src_ref=src, dst_ref=dst, send_sem=send, recv_sem=recv,
            device_id=(dev,), device_id_type=MESH,
        )

    slab = pl.ds(pl.multiple_of(core * T, T), T)
    own = pl.ds(pl.multiple_of(4 * T + core * T, T), T)
    mine8 = pl.ds(HK * core, HK)
    theirs8 = pl.ds(HK * (1 - core), HK)
    mine16 = pl.ds(2 * HK * core, 2 * HK)
    theirs16 = pl.ds(2 * HK * (1 - core), 2 * HK)

    starts = [
        (k_in, mine8, theirs8, kv.at[:, 0, own]),
        (v_in, mine8, theirs8, kv.at[:, 1, own]),
        (q_in, mine16, theirs16, q.at[core]),
        (do_in, mine16, theirs16, do.at[:, :, slab]),
    ]
    local, cross = [], []
    for at, (src, mine, theirs, dst) in enumerate(starts):
        cross.append(remote(src.at[theirs], dst, d2d_send.at[at], d2d_recv.at[at], sib))
        local.append(pltpu.make_async_copy(src.at[mine], dst, loc_sem.at[at]))
        cross[-1].start()
        local[-1].start()

    def to_b(i):
        return remote(
            kv.at[i, :, pl.ds(4 * T, 2 * T)], kv.at[i, :, pl.ds(2 * T, 2 * T)],
            fb_send.at[i], fb_recv.at[i], nxt,
        )

    def to_a(i):
        return remote(
            kv.at[i, :, pl.ds(2 * T, 2 * T)], kv.at[i, :, pl.ds(0, 2 * T)],
            fa_send.at[i], fa_recv.at[i], nxt,
        )

    def back_a(i):
        return remote(part_a.at[i], got_a.at[i], ra_send.at[i], ra_recv.at[i], prv)

    def back_b(i):
        return remote(part_b.at[i], got_b.at[i], rb_send.at[i], rb_recv.at[i], prv)

    def dq_copies(i):
        heads = pl.ds(2 * (HK * core + i), 2)
        return (
            pltpu.make_async_copy(dq.at[core, pl.ds(2 * i, 2)], dq_out.at[heads], out_loc.at[0, i]),
            remote(
                dq.at[1 - core, pl.ds(2 * i, 2)], dq_out.at[heads],
                out_send.at[0, i], out_recv.at[0, i], sib,
            ),
        )

    def dkv_copies(i):
        head = HK * core + i
        other = pl.ds(pl.multiple_of((1 - core) * T, T), T)
        return (
            pltpu.make_async_copy(fin.at[i, :, slab], dkv_out.at[head], out_loc.at[1, i]),
            remote(
                fin.at[i, :, other], dkv_out.at[head], out_send.at[1, i], out_recv.at[1, i], sib
            ),
        )

    for at in (0, 1):
        local[at].wait()
        cross[at].wait_recv()
    for i in range(3):
        to_b(i).start()
    for at in (2, 3):
        local[at].wait()
        cross[at].wait_recv()
    to_b(0).wait_recv()
    to_a(0).start()

    first = 2 * chip - 4

    def back1(i):
        back_a(i).wait_recv()
        part_b[i] = (acc[i, :, 2 * T : 4 * T, :] + got_a[i].astype(jnp.float32)).astype(jnp.bfloat16)
        back_b(i).start()

    def back2(i):
        back_b(i).wait_recv()
        fin[i] = (acc[i, :, 4 * T :, :] + got_b[i].astype(jnp.float32)).astype(jnp.bfloat16)
        for copy in dkv_copies(i):
            copy.start()

    def step(i, carry):
        @pl.when(i + 1 < HK)
        def _():
            to_b(i + 1).wait_recv()
            to_a(i + 1).start()

        @pl.when(i + 3 < HK)
        def _():
            to_b(i + 3).start()

        to_a(i).wait_recv()
        attend(i, first, kv, q, do, s_scr, p_scr, g_scr, ds_scr, acc, dq)
        part_a[i] = acc[i, :, : 2 * T, :].astype(jnp.bfloat16)
        back_a(i).start()
        for copy in dq_copies(i):
            copy.start()

        @pl.when(i >= 1)
        def _():
            back1(i - 1)

        @pl.when(i >= 2)
        def _():
            back2(i - 2)

        return carry

    lax.fori_loop(0, HK, step, 0)
    back1(HK - 1)
    back2(HK - 2)
    back2(HK - 1)

    for copy in cross:
        copy.wait_send()

    def finish(i, carry):
        to_b(i).wait_send()
        to_a(i).wait_send()
        back_a(i).wait_send()
        back_b(i).wait_send()
        for here, there in (dq_copies(i), dkv_copies(i)):
            here.wait()
            there.wait()
        return carry

    lax.fori_loop(0, HK, finish, 0)


def on_device(query_rows, key_rows, value_rows, grad_out):
    n = lax.axis_size("ctx")
    gathered = lax.all_to_all(grad_out, "ctx", split_axis=1, concat_axis=0, tiled=True)
    do_in = gathered.reshape(4 * HK, D, T)
    q_in = jnp.transpose(query_rows, (1, 0, 2))
    k_in = jnp.transpose(key_rows, (1, 0, 2))
    v_in = jnp.transpose(value_rows, (1, 0, 2))
    dma = pltpu.SemaphoreType.DMA
    bf16, f32 = jnp.bfloat16, jnp.float32
    any_spec = pl.BlockSpec(memory_space=pl.ANY)
    dq_heads, dkv = pl.pallas_call(
        functools.partial(kernel, n),
        out_shape=(
            jax.ShapeDtypeStruct((4 * HK, T, D), bf16),
            jax.ShapeDtypeStruct((2 * HK, 2, T, D), bf16),
        ),
        in_specs=[any_spec] * 4,
        out_specs=(any_spec, any_spec),
        scratch_shapes=[
            pltpu.VMEM((HK, 2, 6 * T, D), bf16),
            pltpu.VMEM((2, 2 * HK, T, D), bf16),
            pltpu.VMEM((2 * HK, D, 2 * T), bf16),
            pltpu.VMEM((2, 2 * HK, T, D), bf16),
            pltpu.VMEM((5 * T, 2 * T), f32),
            pltpu.VMEM((5 * T, 2 * T), f32),
            pltpu.VMEM((5 * T, 2 * T), f32),
            pltpu.VMEM((5 * T, 2 * T), bf16),
            pltpu.VMEM((HK, 2, 6 * T, D), f32),
            pltpu.VMEM((HK, 2, 2 * T, D), bf16),
            pltpu.VMEM((HK, 2, 2 * T, D), bf16),
            pltpu.VMEM((HK, 2, 2 * T, D), bf16),
            pltpu.VMEM((HK, 2, 2 * T, D), bf16),
            pltpu.VMEM((HK, 2, 2 * T, D), bf16),
            dma((4,)), dma((4,)), dma((4,)),
            dma((HK,)), dma((HK,)), dma((HK,)), dma((HK,)),
            dma((HK,)), dma((HK,)), dma((HK,)), dma((HK,)),
            dma((2, HK)), dma((2, HK)), dma((2, HK)),
        ],
        compiler_params=pltpu.CompilerParams(
            collective_id=0, has_side_effects=True, vmem_limit_bytes=58 * 2**20
        ),
        cost_estimate=pl.CostEstimate(
            flops=14_000_000_000, bytes_accessed=12 * 2**20, transcendentals=10_000_000
        ),
    )(q_in, k_in, v_in, do_in)
    grad_query = jnp.transpose(dq_heads, (1, 0, 2))
    grad_key = jnp.transpose(dkv[:, 0], (1, 0, 2))
    grad_value = jnp.transpose(dkv[:, 1], (1, 0, 2))
    return (grad_query, grad_key, grad_value)


def solution(mesh):
    in_specs = (P("ctx", None, None), P("ctx", None, None), P("ctx", None, None), P("ctx", None))
    out_specs = (P("ctx", None, None), P("ctx", None, None), P("ctx", None, None))
    return jax.shard_map(
        on_device, mesh=mesh, in_specs=in_specs, out_specs=out_specs, check_vma=False
    )
```

time: 686 us -> 184 us (0.27)
  matrix products: 255 us -> 0 us
  waiting for transfers between devices: 223 us -> 23.5 us
  Pallas kernels: 0 us -> 130 us
  starting transfers between devices: 93.7 us -> 11.2 us
  local copies, waits for them, and re-layouts: 65.2 us -> 15.2 us
  other arithmetic: 44.5 us -> 0 us
    ppermute x16 -> x0, waiting for transfers between devices: 223 us -> none  [from_behind(): return lax.ppermute(value, axis, pairs)]
    dot_general x64 -> x0, matrix products: 200 us -> none  [the longest x16 66.8 us: head_pass(): jnp.einsum('htk,kd->thd', dscores, k_window, preferred_element_type=jnp.f...]
    pallas_call x0 -> x1, Pallas kernels: none -> 130 us  [on_device(): pl.pallas_call(functools.partial(kernel, n), out_shape=(jax.ShapeDtypeStr...]
    ppermute x16 -> x0, starting transfers between devices: 85.6 us -> none  [from_behind(): return lax.ppermute(value, axis, pairs)]
    sub x16 -> x0, matrix products: 55.3 us -> none  [head_pass(): weights = jnp.exp(masked - top)]
    convert_element_type x18 -> x0, other arithmetic: 39.2 us -> none  [the longest x16 31.3 us: head_pass(): (weights / jnp.sum(weights, axis=-1, keepdims=True)).astype(jnp.bfloat16)]
    while x2 -> x0, local copies, waits for them, and re-layouts: 29 us -> none  [on_device(): lax.map(partial(head_pass, allowed), (query_heads, window_keys, window_va...]
    all_to_all x1, waiting for transfers between devices: 0.01 us -> 23.5 us  [on_device(): lax.all_to_all(grad_out, 'ctx', split_axis=1, concat_axis=0, tiled=True)]
  transfers between devices with their start and end apart: 17 -> 1, of which waited for: 10 -> 1; matrix products, arithmetic and copies ran while one was open for 7% -> 2% of each run, Pallas kernels for 0% -> 0%
where the time goes in v1:
time: 184 us; the launch traced here: 181 us
  Pallas kernels  130 us (71%)
  waiting for transfers between devices  23.5 us (13%)
  local copies, waits for them, and re-layouts  15.2 us (8%)
  starting transfers between devices  11.2 us (6%)
    pallas_call x1, Pallas kernels, on_device(): pl.pallas_call(functools.partial(kernel, n), out_shape=(jax.ShapeDtypeStr...  130 us
    all_to_all x1, waiting for transfers between devices, on_device(): lax.all_to_all(grad_out, 'ctx', split_axis=1, concat_axis=0, tiled=True)  23.5 us
    all_to_all x1, starting transfers between devices, on_device(): lax.all_to_all(grad_out, 'ctx', split_axis=1, concat_axis=0, tiled=True)  11.2 us
    unnamed x12, local copies, waits for them, and re-layouts  9.86 us
  transfers between devices with their start and end apart: 1, of which 1 were waited for; matrix products, arithmetic and copies ran while one was open for 2% of the time, Pallas kernels for 0%

profile of v1, /device:TPU:7, one launch (start us, length us, event | category | flops | bytes accessed | tf_op | source)
XLA Modules:
  0.0 180.5 jit_solution(14134449053912587605)
XLA Ops:
  0.6 3.2 %copy.19 = bf16[4,128,8,256]{3,2,0,1:T(8,128)(2,1)} copy(bf16[4,128,8,256]{3,2,1,0:T(8,128)(2,1)} %bitcast.23) | data formatting | bytes 4194304 | tf_op jit(solution)/shard_map/all_to_all | solution.py:243
  3.8 0.0 copy-start
  3.8 11.2 %all-to-all-start = ((bf16[32,128,256]{2,0,1:T(8,128)(2,1)}), bf16[32,128,256]{2,0,1:T(8,128)(2,1)}, u32[]{:S(2)}, u32[]{:S(2)}) async-start(bf16[32,128,256]{2,0,1:T(8,128)(2,1)} %bitcast.21), calls=%async_computation | async-start | bytes 4194304 | tf_op jit(solution)/shard_map/all_to_all | solution.py:243
  15.1 0.0 copy-done
  15.1 0.0 copy-start.2
  15.1 0.0 copy-start.3
  15.1 2.1 %copy.20 = bf16[256,32,128]{2,0,1:T(8,128)(2,1)} copy(bf16[256,32,128]{2,1,0:T(8,128)(2,1)S(1)} %copy-done) | data formatting | bytes 4194304 | tf_op args[0]
  17.2 0.0 copy-done.2
  17.2 0.0 copy-done.3
  17.2 1.9 %copy_bitcast_fusion.2 = (bf16[16,256,128]{2,1,0:T(8,128)(2,1)}, bf16[16,256,128]{2,1,0:T(8,128)(2,1)}) fusion(bf16[256,16,128]{2,1,0:T(8,128)(2,1)S(1)} %copy-done.2, bf16[256,16,128]{2,1,0:T(8,128)(2,1)S(1)} %copy-done.3), kind=kLoop, calls=%fused_computation.2 | loop fusion | bytes 4194304 | tf_op jit(solution)/shard_map/transpose | solution.py:247
  19.2 23.5 %all-to-all-done = bf16[32,128,256]{2,0,1:T(8,128)(2,1)} async-done(((bf16[32,128,256]{2,0,1:T(8,128)(2,1)}), bf16[32,128,256]{2,0,1:T(8,128)(2,1)}, u32[]{:S(2)}, u32[]{:S(2)}) %all-to-all-start) | async-done | bytes 2097184 | tf_op jit(solution)/shard_map/all_to_all | solution.py:243
  42.6 129.9 %shard_map.67 = (bf16[32,256,128]{2,1,0:T(8,128)(2,1)}, bf16[16,2,256,128]{3,2,1,0:T(8,128)(2,1)}) custom-call(bf16[32,256,128]{2,1,0:T(8,128)(2,1)} %bitcast.24, bf16[16,256,128]{2,1,0:T(8,128)(2,1)} %get-tuple-element.13.k_in, bf16[16,256,128]{2,1,0:T(8,128)(2,1)} %get-tuple-element.12.v_in, bf16[32,128,256]{2,1,0:T(8,128)(2,1)} %bitcast.4.do_in), custom_call_target="tpu_custom_call" | custom-call | flops 14000000000 | bytes 12582912 | tf_op jit(solution)/shard_map/pallas_call | solution.py:251
  172.6 0.0 copy-start.1
  172.6 4.4 %copy.11 = bf16[256,32,128]{2,1,0:T(8,128)(2,1)} copy(bf16[256,32,128]{2,0,1:T(8,128)(2,1)} %bitcast.25) | data formatting | bytes 4194304
  177.0 0.0 copy-done.1
  177.0 0.2 slice_bitcast_fusion
  177.2 1.7 copy.13
  178.9 1.6 copy.12
Async XLA Ops:
  3.8 11.3 %copy-start = (bf16[256,32,128]{2,1,0:T(8,128)(2,1)S(1)}, bf16[256,32,128]{2,1,0:T(8,128)(2,1)}, u32[]{:S(2)}) copy-start(bf16[256,32,128]{2,1,0:T(8,128)(2,1)} %param.4) | copy-start | bytes 6291460
  3.8 38.8 %all-to-all-start = ((bf16[32,128,256]{2,0,1:T(8,128)(2,1)}), bf16[32,128,256]{2,0,1:T(8,128)(2,1)}, u32[]{:S(2)}, u32[]{:S(2)}) async-start(bf16[32,128,256]{2,0,1:T(8,128)(2,1)} %bitcast.21), calls=%async_computation | async-start | bytes 4194304 | tf_op jit(solution)/shard_map/all_to_all | solution.py:243
  15.1 2.2 %copy-start.2 = (bf16[256,16,128]{2,1,0:T(8,128)(2,1)S(1)}, bf16[256,16,128]{2,1,0:T(8,128)(2,1)}, u32[]{:S(2)}) copy-start(bf16[256,16,128]{2,1,0:T(8,128)(2,1)} %param.6) | copy-start | bytes 3145732
  15.1 2.1 %copy-start.3 = (bf16[256,16,128]{2,1,0:T(8,128)(2,1)S(1)}, bf16[256,16,128]{2,1,0:T(8,128)(2,1)}, u32[]{:S(2)}) copy-start(bf16[256,16,128]{2,1,0:T(8,128)(2,1)} %param.5) | copy-start | bytes 3145732
  172.6 4.4 %copy-start.1 = (bf16[16,2,256,128]{3,2,1,0:T(8,128)(2,1)S(1)}, bf16[16,2,256,128]{3,2,1,0:T(8,128)(2,1)}, u32[]{:S(2)}) copy-start(bf16[16,2,256,128]{3,2,1,0:T(8,128)(2,1)} %get-tuple-element.6) | copy-start | bytes 6291460

commit v2 on v1

--- a/solution.py
+++ b/solution.py
@@ -88,7 +88,7 @@
     kv, q, do, dq, s_scr, p_scr, g_scr, ds_scr, acc,
     part_a, got_a, part_b, got_b, fin,
     loc_sem, d2d_send, d2d_recv, fb_send, fb_recv, fa_send, fa_recv,
-    ra_send, ra_recv, rb_send, rb_recv, out_loc, out_send, out_recv,
+    ra_send, ra_recv, rb_send, rb_recv, out_loc, out_send, out_recv, go_send, go_recv,
 ):
     me = lax.axis_index("ctx")
     core = lax.rem(me, 2)
@@ -97,16 +97,11 @@
     nxt = lax.rem(me + 2, n)
     prv = lax.rem(me + n - 2, n)
 
-    barrier = pltpu.get_barrier_semaphore()
-    for other in (sib, nxt, prv):
-        pl.semaphore_signal(barrier, inc=1, device_id=(other,), device_id_type=MESH)
-    pl.semaphore_wait(barrier, 3)
-
-    def remote(src, dst, send, recv, dev):
-        return pltpu.make_async_remote_copy(
-            src_ref=src, dst_ref=dst, send_sem=send, recv_sem=recv,
-            device_id=(dev,), device_id_type=MESH,
-        )
+    chips = n // 2
+    worker = me // chips
+    head = lax.rem(me // 4, 2 * HK)
+    quarter = lax.rem(me, 4)
+    stays = worker == core
 
     slab = pl.ds(pl.multiple_of(core * T, T), T)
     own = pl.ds(pl.multiple_of(4 * T + core * T, T), T)
@@ -119,14 +114,58 @@
         (k_in, mine8, theirs8, kv.at[:, 0, own]),
         (v_in, mine8, theirs8, kv.at[:, 1, own]),
         (q_in, mine16, theirs16, q.at[core]),
-        (do_in, mine16, theirs16, do.at[:, :, slab]),
     ]
-    local, cross = [], []
-    for at, (src, mine, theirs, dst) in enumerate(starts):
+    local = []
+    for at, (src, mine, _, dst) in enumerate(starts):
+        local.append(pltpu.make_async_copy(src.at[mine], dst, loc_sem.at[at]))
+        local[-1].start()
+
+    barrier = pltpu.get_barrier_semaphore()
+    for other in (sib, nxt, prv):
+        pl.semaphore_signal(barrier, inc=1, device_id=(other,), device_id_type=MESH)
+
+    def greet(i, carry):
+        sender = chips * core + i
+
+        @pl.when(sender != me)
+        def _():
+            pl.semaphore_signal(barrier, inc=1, device_id=(sender,), device_id_type=MESH)
+
+        return carry
+
+    lax.fori_loop(0, chips, greet, 0)
+    pl.semaphore_wait(barrier, 3 + chips - jnp.where(stays, 1, 0))
+
+    def remote(src, dst, send, recv, dev):
+        return pltpu.make_async_remote_copy(
+            src_ref=src, dst_ref=dst, send_sem=send, recv_sem=recv,
+            device_id=(dev,), device_id_type=MESH,
+        )
+
+    cross = []
+    for at, (src, _, theirs, dst) in enumerate(starts):
         cross.append(remote(src.at[theirs], dst, d2d_send.at[at], d2d_recv.at[at], sib))
-        local.append(pltpu.make_async_copy(src.at[mine], dst, loc_sem.at[at]))
         cross[-1].start()
-        local[-1].start()
+
+    def piece(i):
+        to = lax.rem(chip + 21 * i, chips)
+        return (
+            do_in.at[:, pl.ds(pl.multiple_of(to * 2 * T, 2 * T), 2 * T)],
+            do.at[head, pl.ds(pl.multiple_of(quarter * 32, 32), 32), :],
+            2 * to + worker,
+        )
+
+    def spread(i):
+        src, dst, dev = piece(i)
+        return remote(src, dst, go_send.at[i], go_recv.at[head], dev)
+
+    def keep():
+        src, dst, _ = piece(0)
+        return pltpu.make_async_copy(src, dst, go_recv.at[head])
+
+    def spread_start(i, carry):
+        spread(i).start()
+        return carry
 
     def to_b(i):
         return remote(
@@ -166,14 +205,22 @@
             ),
         )
 
+    @pl.when(stays)
+    def _():
+        keep().start()
+
+    @pl.when(jnp.logical_not(stays))
+    def _():
+        spread(0).start()
+
+    lax.fori_loop(1, chips, spread_start, 0)
     for at in (0, 1):
         local[at].wait()
         cross[at].wait_recv()
     for i in range(3):
         to_b(i).start()
-    for at in (2, 3):
-        local[at].wait()
-        cross[at].wait_recv()
+    local[2].wait()
+    cross[2].wait_recv()
     to_b(0).wait_recv()
     to_a(0).start()
 
@@ -201,6 +248,8 @@
             to_b(i + 3).start()
 
         to_a(i).wait_recv()
+        for h in range(2):
+            pltpu.make_async_copy(do.at[2 * i + h], do.at[2 * i + h], go_recv.at[2 * i + h]).wait()
         attend(i, first, kv, q, do, s_scr, p_scr, g_scr, ds_scr, acc, dq)
         part_a[i] = acc[i, :, : 2 * T, :].astype(jnp.bfloat16)
         back_a(i).start()
@@ -237,11 +286,19 @@
 
     lax.fori_loop(0, HK, finish, 0)
 
+    @pl.when(jnp.logical_not(stays))
+    def _():
+        spread(0).wait_send()
+
+    def spread_done(i, carry):
+        spread(i).wait_send()
+        return carry
+
+    lax.fori_loop(1, chips, spread_done, 0)
+
 
 def on_device(query_rows, key_rows, value_rows, grad_out):
     n = lax.axis_size("ctx")
-    gathered = lax.all_to_all(grad_out, "ctx", split_axis=1, concat_axis=0, tiled=True)
-    do_in = gathered.reshape(4 * HK, D, T)
     q_in = jnp.transpose(query_rows, (1, 0, 2))
     k_in = jnp.transpose(key_rows, (1, 0, 2))
     v_in = jnp.transpose(value_rows, (1, 0, 2))
@@ -271,10 +328,11 @@
             pltpu.VMEM((HK, 2, 2 * T, D), bf16),
             pltpu.VMEM((HK, 2, 2 * T, D), bf16),
             pltpu.VMEM((HK, 2, 2 * T, D), bf16),
-            dma((4,)), dma((4,)), dma((4,)),
+            dma((3,)), dma((3,)), dma((3,)),
             dma((HK,)), dma((HK,)), dma((HK,)), dma((HK,)),
             dma((HK,)), dma((HK,)), dma((HK,)), dma((HK,)),
             dma((2, HK)), dma((2, HK)), dma((2, HK)),
+            dma((n // 2,)), dma((2 * HK,)),
         ],
         compiler_params=pltpu.CompilerParams(
             collective_id=0, has_side_effects=True, vmem_limit_bytes=58 * 2**20
@@ -282,7 +340,7 @@
         cost_estimate=pl.CostEstimate(
             flops=14_000_000_000, bytes_accessed=12 * 2**20, transcendentals=10_000_000
         ),
-    )(q_in, k_in, v_in, do_in)
+    )(q_in, k_in, v_in, grad_out)
     grad_query = jnp.transpose(dq_heads, (1, 0, 2))
     grad_key = jnp.transpose(dkv[:, 0], (1, 0, 2))
     grad_value = jnp.transpose(dkv[:, 1], (1, 0, 2))

time: 184 us -> 172 us (0.935); the launches traced: 181 us -> 172 us
  Pallas kernels: 130 us -> 158 us
  waiting for transfers between devices: 23.5 us -> 0 us
  starting transfers between devices: 11.2 us -> 0 us
    pallas_call x1, Pallas kernels: 130 us -> 158 us  [on_device(): pl.pallas_call(functools.partial(kernel, n), out_shape=(jax.ShapeDtypeStr...]
    all_to_all x1 -> x0, waiting for transfers between devices: 23.5 us -> none  [on_device(): lax.all_to_all(grad_out, 'ctx', split_axis=1, concat_axis=0, tiled=True)]
    all_to_all x1 -> x0, starting transfers between devices: 11.2 us -> none  [on_device(): lax.all_to_all(grad_out, 'ctx', split_axis=1, concat_axis=0, tiled=True)]
    all_to_all x1 -> x0, local copies, waits for them, and re-layouts: 3.19 us -> none  [on_device(): lax.all_to_all(grad_out, 'ctx', split_axis=1, concat_axis=0, tiled=True)]
    unnamed x12 -> x10, local copies, waits for them, and re-layouts: 9.86 us -> 11.6 us
  transfers between devices with their start and end apart: 1 -> 0, of which waited for: 1 -> 0; matrix products, arithmetic and copies ran while one was open for 2% -> 0% of each run, Pallas kernels for 0% -> 0%
where the time goes in v2:
time: 172 us
  Pallas kernels  158 us (92%)
  local copies, waits for them, and re-layouts  13.7 us (8%)
    pallas_call x1, Pallas kernels, on_device(): pl.pallas_call(functools.partial(kernel, n), out_shape=(jax.ShapeDtypeStr...  158 us
    unnamed x10, local copies, waits for them, and re-layouts  11.6 us

profile of v2, /device:TPU:7, one launch (start us, length us, event | category | flops | bytes accessed | tf_op | source)
XLA Modules:
  0.0 172.0 jit_solution(16653584970233748438)
XLA Ops:
  0.6 0.0 copy-start.1
  0.6 0.0 copy-start.2
  0.7 3.9 %copy.16 = bf16[256,32,128]{2,0,1:T(8,128)(2,1)} copy(bf16[256,32,128]{2,1,0:T(8,128)(2,1)} %param.4) | data formatting | bytes 4194304 | tf_op args[0]
  4.5 0.0 copy-done.1
  4.5 0.0 copy-done.2
  4.5 1.9 %copy_bitcast_fusion.1 = (bf16[16,256,128]{2,1,0:T(8,128)(2,1)}, bf16[16,256,128]{2,1,0:T(8,128)(2,1)}) fusion(bf16[256,16,128]{2,1,0:T(8,128)(2,1)S(1)} %copy-done.1, bf16[256,16,128]{2,1,0:T(8,128)(2,1)S(1)} %copy-done.2), kind=kLoop, calls=%fused_computation.1 | loop fusion | bytes 4194304 | tf_op jit(solution)/shard_map/transpose | solution.py:304
  6.5 157.6 %shard_map.67 = (bf16[32,256,128]{2,1,0:T(8,128)(2,1)}, bf16[16,2,256,128]{3,2,1,0:T(8,128)(2,1)}) custom-call(bf16[32,256,128]{2,1,0:T(8,128)(2,1)} %bitcast.16, bf16[16,256,128]{2,1,0:T(8,128)(2,1)} %get-tuple-element.13.k_in, bf16[16,256,128]{2,1,0:T(8,128)(2,1)} %get-tuple-element.12.v_in, bf16[32,32768]{1,0:T(8,128)(2,1)} %do_in.1), custom_call_target="tpu_custom_call" | custom-call | flops 14000000000 | bytes 12582912 | tf_op jit(solution)/shard_map/pallas_call | solution.py:308
  164.1 0.0 copy-start
  164.1 4.4 %copy.10 = bf16[256,32,128]{2,1,0:T(8,128)(2,1)} copy(bf16[256,32,128]{2,0,1:T(8,128)(2,1)} %bitcast.17) | data formatting | bytes 4194304
  168.5 0.0 copy-done
  168.5 0.2 slice_bitcast_fusion
  168.7 1.7 copy.12
  170.4 1.6 copy.11
Async XLA Ops:
  0.6 3.9 %copy-start.1 = (bf16[256,16,128]{2,1,0:T(8,128)(2,1)S(1)}, bf16[256,16,128]{2,1,0:T(8,128)(2,1)}, u32[]{:S(2)}) copy-start(bf16[256,16,128]{2,1,0:T(8,128)(2,1)} %param.6) | copy-start | bytes 3145732
  0.6 3.9 %copy-start.2 = (bf16[256,16,128]{2,1,0:T(8,128)(2,1)S(1)}, bf16[256,16,128]{2,1,0:T(8,128)(2,1)}, u32[]{:S(2)}) copy-start(bf16[256,16,128]{2,1,0:T(8,128)(2,1)} %param.5) | copy-start | bytes 3145732
  164.1 4.4 %copy-start = (bf16[16,2,256,128]{3,2,1,0:T(8,128)(2,1)S(1)}, bf16[16,2,256,128]{3,2,1,0:T(8,128)(2,1)}, u32[]{:S(2)}) copy-start(bf16[16,2,256,128]{3,2,1,0:T(8,128)(2,1)} %get-tuple-element.6) | copy-start | bytes 6291460

commit v3 on v2

--- a/solution.py
+++ b/solution.py
@@ -85,6 +85,7 @@
 
 def kernel(
     n, q_in, k_in, v_in, do_in, dq_out, dkv_out,
+    q_raw, k_raw, v_raw, q_heads, kv_heads,
     kv, q, do, dq, s_scr, p_scr, g_scr, ds_scr, acc,
     part_a, got_a, part_b, got_b, fin,
     loc_sem, d2d_send, d2d_recv, fb_send, fb_recv, fa_send, fa_recv,
@@ -105,19 +106,9 @@
 
     slab = pl.ds(pl.multiple_of(core * T, T), T)
     own = pl.ds(pl.multiple_of(4 * T + core * T, T), T)
-    mine8 = pl.ds(HK * core, HK)
-    theirs8 = pl.ds(HK * (1 - core), HK)
-    mine16 = pl.ds(2 * HK * core, 2 * HK)
-    theirs16 = pl.ds(2 * HK * (1 - core), 2 * HK)
-
-    starts = [
-        (k_in, mine8, theirs8, kv.at[:, 0, own]),
-        (v_in, mine8, theirs8, kv.at[:, 1, own]),
-        (q_in, mine16, theirs16, q.at[core]),
-    ]
     local = []
-    for at, (src, mine, _, dst) in enumerate(starts):
-        local.append(pltpu.make_async_copy(src.at[mine], dst, loc_sem.at[at]))
+    for at, (src, dst) in enumerate(((k_in, k_raw), (v_in, v_raw), (q_in, q_raw))):
+        local.append(pltpu.make_async_copy(src, dst, loc_sem.at[at]))
         local[-1].start()
 
     barrier = pltpu.get_barrier_semaphore()
@@ -141,11 +132,6 @@
             src_ref=src, dst_ref=dst, send_sem=send, recv_sem=recv,
             device_id=(dev,), device_id_type=MESH,
         )
-
-    cross = []
-    for at, (src, _, theirs, dst) in enumerate(starts):
-        cross.append(remote(src.at[theirs], dst, d2d_send.at[at], d2d_recv.at[at], sib))
-        cross[-1].start()
 
     def piece(i):
         to = lax.rem(chip + 21 * i, chips)
@@ -214,13 +200,45 @@
         spread(0).start()
 
     lax.fori_loop(1, chips, spread_start, 0)
-    for at in (0, 1):
-        local[at].wait()
-        cross[at].wait_recv()
+    moves = [
+        (kv_heads.at[core], kv_heads.at[1 - core], kv.at[:, :, own]),
+        (q_heads.at[core], q_heads.at[1 - core], q.at[core]),
+    ]
+    cross, keeps = [], []
+    for at, (mine, theirs, dst) in enumerate(moves):
+        cross.append(remote(theirs, dst, d2d_send.at[at], d2d_recv.at[at], sib))
+        keeps.append(pltpu.make_async_copy(mine, dst, loc_sem.at[3 + at]))
+
+    def turn_kv(i, carry):
+        rows = pl.ds(pl.multiple_of(i * 16, 16), 16)
+        for at, raw in enumerate((k_raw, v_raw)):
+            turned = jnp.swapaxes(raw[rows], 0, 1)
+            for half in range(2):
+                kv_heads[half, :, at, rows, :] = turned[half * HK : (half + 1) * HK]
+        return carry
+
+    def turn_q(i, carry):
+        rows = pl.ds(pl.multiple_of(i * 16, 16), 16)
+        turned = jnp.swapaxes(q_raw[rows], 0, 1)
+        for half in range(2):
+            q_heads[half, :, rows, :] = turned[half * 2 * HK : (half + 1) * 2 * HK]
+        return carry
+
+    local[0].wait()
+    local[1].wait()
+    lax.fori_loop(0, T // 16, turn_kv, 0)
+    cross[0].start()
+    keeps[0].start()
+    keeps[0].wait()
+    cross[0].wait_recv()
     for i in range(3):
         to_b(i).start()
     local[2].wait()
-    cross[2].wait_recv()
+    lax.fori_loop(0, T // 16, turn_q, 0)
+    cross[1].start()
+    keeps[1].start()
+    keeps[1].wait()
+    cross[1].wait_recv()
     to_b(0).wait_recv()
     to_a(0).start()
 
@@ -297,11 +315,16 @@
     lax.fori_loop(1, chips, spread_done, 0)
 
 
+def turn_back(dq_ref, dkv_ref, gq_ref, gk_ref, gv_ref):
+    for r in range(0, dq_ref.shape[1], 16):
+        rows = pl.ds(r, 16)
+        gq_ref[rows] = jnp.swapaxes(dq_ref[:, rows, :], 0, 1)
+        gk_ref[rows] = jnp.swapaxes(dkv_ref[:, 0, rows, :], 0, 1)
+        gv_ref[rows] = jnp.swapaxes(dkv_ref[:, 1, rows, :], 0, 1)
+
+
 def on_device(query_rows, key_rows, value_rows, grad_out):
     n = lax.axis_size("ctx")
-    q_in = jnp.transpose(query_rows, (1, 0, 2))
-    k_in = jnp.transpose(key_rows, (1, 0, 2))
-    v_in = jnp.transpose(value_rows, (1, 0, 2))
     dma = pltpu.SemaphoreType.DMA
     bf16, f32 = jnp.bfloat16, jnp.float32
     any_spec = pl.BlockSpec(memory_space=pl.ANY)
@@ -314,6 +337,11 @@
         in_specs=[any_spec] * 4,
         out_specs=(any_spec, any_spec),
         scratch_shapes=[
+            pltpu.VMEM((T, 4 * HK, D), bf16),
+            pltpu.VMEM((T, 2 * HK, D), bf16),
+            pltpu.VMEM((T, 2 * HK, D), bf16),
+            pltpu.VMEM((2, 2 * HK, T, D), bf16),
+            pltpu.VMEM((2, HK, 2, T, D), bf16),
             pltpu.VMEM((HK, 2, 6 * T, D), bf16),
             pltpu.VMEM((2, 2 * HK, T, D), bf16),
             pltpu.VMEM((2 * HK, D, 2 * T), bf16),
@@ -328,7 +356,7 @@
             pltpu.VMEM((HK, 2, 2 * T, D), bf16),
             pltpu.VMEM((HK, 2, 2 * T, D), bf16),
             pltpu.VMEM((HK, 2, 2 * T, D), bf16),
-            dma((3,)), dma((3,)), dma((3,)),
+            dma((5,)), dma((2,)), dma((2,)),
             dma((HK,)), dma((HK,)), dma((HK,)), dma((HK,)),
             dma((HK,)), dma((HK,)), dma((HK,)), dma((HK,)),
             dma((2, HK)), dma((2, HK)), dma((2, HK)),
@@ -340,11 +368,26 @@
         cost_estimate=pl.CostEstimate(
             flops=14_000_000_000, bytes_accessed=12 * 2**20, transcendentals=10_000_000
         ),
-    )(q_in, k_in, v_in, grad_out)
-    grad_query = jnp.transpose(dq_heads, (1, 0, 2))
-    grad_key = jnp.transpose(dkv[:, 0], (1, 0, 2))
-    grad_value = jnp.transpose(dkv[:, 1], (1, 0, 2))
-    return (grad_query, grad_key, grad_value)
+    )(query_rows, key_rows, value_rows, grad_out)
+    rows = 64
+    return pl.pallas_call(
+        turn_back,
+        grid=(T // rows,),
+        out_shape=(
+            jax.ShapeDtypeStruct(query_rows.shape, bf16),
+            jax.ShapeDtypeStruct(key_rows.shape, bf16),
+            jax.ShapeDtypeStruct(value_rows.shape, bf16),
+        ),
+        in_specs=[
+            pl.BlockSpec((4 * HK, rows, D), lambda i: (0, i, 0)),
+            pl.BlockSpec((2 * HK, 2, rows, D), lambda i: (0, 0, i, 0)),
+        ],
+        out_specs=(
+            pl.BlockSpec((rows, 4 * HK, D), lambda i: (i, 0, 0)),
+            pl.BlockSpec((rows, 2 * HK, D), lambda i: (i, 0, 0)),
+            pl.BlockSpec((rows, 2 * HK, D), lambda i: (i, 0, 0)),
+        ),
+    )(dq_heads, dkv)
 
 
 def solution(mesh):

time: 172 us -> 164 us (0.953)
  local copies, waits for them, and re-layouts: 13.7 us -> 0 us
  Pallas kernels: 158 us -> 163 us
    unnamed x10 -> x0, local copies, waits for them, and re-layouts: 11.6 us -> none
    pallas_call x0 -> x1, Pallas kernels: none -> 4.96 us  [on_device(): pl.pallas_call(turn_back, grid=(T // rows,), out_shape=(jax.ShapeDtypeStr...]
    transpose x2 -> x0, local copies, waits for them, and re-layouts: 2.15 us -> none  [the longest x1 1.94 us: on_device(): v_in = jnp.transpose(value_rows, (1, 0, 2))]
where the time goes in v3:
time: 164 us; the launch traced here: 163 us
  Pallas kernels  163 us (99%)
    pallas_call x1, Pallas kernels, on_device(): pl.pallas_call(functools.partial(kernel, n), out_shape=(jax.ShapeDtypeStr...  158 us
    pallas_call x1, Pallas kernels, on_device(): pl.pallas_call(turn_back, grid=(T // rows,), out_shape=(jax.ShapeDtypeStr...  4.96 us

profile of v3, /device:TPU:7, one launch (start us, length us, event | category | flops | bytes accessed | tf_op | source)
XLA Modules:
  0.0 163.4 jit_solution(7719587035221507596)
XLA Ops:
  0.6 157.8 %shard_map.67 = (bf16[32,256,128]{2,1,0:T(8,128)(2,1)}, bf16[16,2,256,128]{3,2,1,0:T(8,128)(2,1)}) custom-call(bf16[256,32,128]{2,1,0:T(8,128)(2,1)} %q_in.1, bf16[256,16,128]{2,1,0:T(8,128)(2,1)} %k_in.1, bf16[256,16,128]{2,1,0:T(8,128)(2,1)} %v_in.1, bf16[32,32768]{1,0:T(8,128)(2,1)} %do_in.1), custom_call_target="tpu_custom_call" | custom-call | flops 14000000000 | bytes 12582912 | tf_op jit(solution)/shard_map/pallas_call | solution.py:331
  158.4 5.0 %shard_map.68 = (bf16[256,32,128]{2,1,0:T(8,128)(2,1)}, bf16[256,16,128]{2,1,0:T(8,128)(2,1)}, bf16[256,16,128]{2,1,0:T(8,128)(2,1)}) custom-call(bf16[32,256,128]{2,1,0:T(8,128)(2,1)} %get-tuple-element.5.dq_ref, bf16[16,2,256,128]{3,2,1,0:T(8,128)(2,1)} %get-tuple-element.6.dkv_ref), custom_call_target="tpu_custom_call" | custom-call | tf_op jit(solution)/shard_map/pallas_call | solution.py:373

commit v4 on v3

--- a/solution.py
+++ b/solution.py
@@ -369,7 +369,7 @@
             flops=14_000_000_000, bytes_accessed=12 * 2**20, transcendentals=10_000_000
         ),
     )(query_rows, key_rows, value_rows, grad_out)
-    rows = 64
+    rows = 128
     return pl.pallas_call(
         turn_back,
         grid=(T // rows,),

time: 164 us -> 163 us (level)
  no operation moved by 1% of the time
where the time goes in v4:
time: 163 us; the launch traced here: 162 us
  Pallas kernels  162 us (99%)
    pallas_call x1, Pallas kernels, on_device(): pl.pallas_call(functools.partial(kernel, n), out_shape=(jax.ShapeDtypeStr...  158 us
    pallas_call x1, Pallas kernels, on_device(): pl.pallas_call(turn_back, grid=(T // rows,), out_shape=(jax.ShapeDtypeStr...  4.02 us

profile of v4, /device:TPU:7, one launch (start us, length us, event | category | flops | bytes accessed | tf_op | source)
XLA Modules:
  0.0 162.4 jit_solution(1968387408868641745)
XLA Ops:
  0.6 157.8 %shard_map.67 = (bf16[32,256,128]{2,1,0:T(8,128)(2,1)}, bf16[16,2,256,128]{3,2,1,0:T(8,128)(2,1)}) custom-call(bf16[256,32,128]{2,1,0:T(8,128)(2,1)} %q_in.1, bf16[256,16,128]{2,1,0:T(8,128)(2,1)} %k_in.1, bf16[256,16,128]{2,1,0:T(8,128)(2,1)} %v_in.1, bf16[32,32768]{1,0:T(8,128)(2,1)} %do_in.1), custom_call_target="tpu_custom_call" | custom-call | flops 14000000000 | bytes 12582912 | tf_op jit(solution)/shard_map/pallas_call | solution.py:331
  158.4 4.0 %shard_map.68 = (bf16[256,32,128]{2,1,0:T(8,128)(2,1)}, bf16[256,16,128]{2,1,0:T(8,128)(2,1)}, bf16[256,16,128]{2,1,0:T(8,128)(2,1)}) custom-call(bf16[32,256,128]{2,1,0:T(8,128)(2,1)} %get-tuple-element.5.dq_ref, bf16[16,2,256,128]{3,2,1,0:T(8,128)(2,1)} %get-tuple-element.6.dkv_ref), custom_call_target="tpu_custom_call" | custom-call | tf_op jit(solution)/shard_map/pallas_call | solution.py:373
